TPU v7x, 32 devices: a whole 2x2x4 slice. The times are simulated.
32 devices in a mesh: dp: 2 (over x), tensor: 4 (over y, core), section: 4 (over z).
Axes of the slice: x: 2, y: 2, z: 4, core: 2. Of those that a mesh axis runs over, the one named last changes fastest.
Arguments:
- grads: bfloat16 [2, 8, 768, 768], P('dp', 'section', 'tensor'), may hold values from -3 to 3
- owner: int32 [8, 1], P('section'), may hold values from 0 to 1; in each aligned block of 2 rows (0 to 1, 2 to 3, ...) at most 2 rows name the same one
- left_stat: float32 [2, 4, 2, 768, 768], P('dp', 'section', None, 'tensor')
- right_stat: float32 [2, 4, 2, 768, 768], P('dp', 'section', None, 'tensor')
- second_moment: float32 [2, 4, 2, 768, 768], P('dp', 'section', None, 'tensor'), may hold values from 0.05 to 4.5
- left_root: bfloat16 [2, 4, 2, 768, 768], P('dp', 'section', None, 'tensor')
- right_root: bfloat16 [2, 4, 2, 768, 768], P('dp', 'section', None, 'tensor')
Outputs:
- left_new: float32 [2, 4, 2, 768, 768], P('dp', 'section', None, 'tensor')
- right_new: float32 [2, 4, 2, 768, 768], P('dp', 'section', None, 'tensor')
- second_new: float32 [2, 4, 2, 768, 768], P('dp', 'section', None, 'tensor')
- direction: bfloat16 [2, 4, 2, 768, 768], P('dp', 'section', None, 'tensor')
Inputs may be any that keep to these rules, and one draw needn't show every extreme that they name: `owner`: among the 2 blocks of one section, no dp rank owns more than 2.
All inputs are finite; a program needn't handle non-finite values.
Results may differ from a plain program's by a relative error of at most 0.02.
Values may be sent and summed in bfloat16 or wider, within the bound.
A program may use at most 128 MiB of HBM per device.

v0:
```python
import jax
import jax.numpy as jnp
from jax import lax
from jax.sharding import PartitionSpec as P

CAP = 2


def per_device(grads, owner, left_stat, right_stat, second_moment, left_root, right_root):
    block_count = owner.shape[0]
    my_rank = lax.axis_index("dp")
    owners_list = owner[:, 0]
    positions = jnp.arange(block_count, dtype=jnp.int32)
    same_owner = owners_list[:, None] == owners_list[None, :]
    earlier = positions[None, :] < positions[:, None]
    ranked = jnp.sum((same_owner & earlier).astype(jnp.int32), axis=1)
    slot_ids = jnp.arange(CAP, dtype=jnp.int32)
    local_grads = grads[0]
    chosen = (owners_list[None, :] == my_rank) & (ranked[None, :] == slot_ids[:, None])
    index_table = jnp.sum(chosen.astype(jnp.int32) * positions[None, :], axis=1)
    occupied = jnp.any(chosen, axis=1).astype(jnp.float32)
    summed = lax.psum(local_grads.astype(jnp.float32).astype(jnp.bfloat16), "dp").astype(
        jnp.float32
    )
    slot_sum = jnp.take(summed, index_table, axis=0) * occupied[:, None, None]
    gradient = slot_sum.astype(jnp.bfloat16)
    gathered = lax.all_gather(gradient, "tensor", axis=1, tiled=True)
    left_incr = jnp.einsum("cik,cjk->cij", gradient, gathered, preferred_element_type=jnp.float32)
    left_new = 0.95 * left_stat[0, 0] + 0.05 * left_incr
    partials = jnp.einsum("cki,ckj->cij", gradient, gradient, preferred_element_type=jnp.float32)
    right_incr = lax.psum_scatter(
        partials.astype(jnp.bfloat16), "tensor", scatter_dimension=1, tiled=True
    ).astype(jnp.float32)
    right_new = 0.95 * right_stat[0, 0] + 0.05 * right_incr
    grad_wide = gradient.astype(jnp.float32)
    second_new = 0.9 * second_moment[0, 0] + 0.1 * grad_wide * grad_wide
    adam_dir = grad_wide / (jnp.sqrt(second_new) + 1e-08)
    mixed = jnp.einsum(
        "cik,ckj->cij", left_root[0, 0], gathered, preferred_element_type=jnp.float32
    ).astype(jnp.bfloat16)
    precond = jnp.einsum(
        "cik,ckj->cij",
        mixed,
        lax.all_gather(right_root[0, 0], "tensor", axis=1, tiled=True),
        preferred_element_type=jnp.float32,
    )
    precond_sq = jnp.sum(precond * precond, axis=(1, 2))
    adam_sq = jnp.sum(adam_dir * adam_dir, axis=(1, 2))
    precond_sq, adam_sq = lax.psum((precond_sq, adam_sq), "tensor")
    scaling = jnp.sqrt(adam_sq) / jnp.sqrt(precond_sq + 1e-06)
    direction = (precond * scaling[:, None, None]).astype(jnp.bfloat16)
    return (
        left_new[None, None],
        right_new[None, None],
        second_new[None, None],
        direction[None, None],
    )


def solution(mesh):
    placed = (
        P("dp", "section", "tensor", None),
        P("section", None),
        P("dp", "section", None, "tensor", None),
        P("dp", "section", None, "tensor", None),
        P("dp", "section", None, "tensor", None),
        P("dp", "section", None, "tensor", None),
        P("dp", "section", None, "tensor", None),
    )
    return jax.shard_map(
        per_device,
        mesh=mesh,
        in_specs=placed,
        out_specs=(
            P("dp", "section", None, "tensor", None),
            P("dp", "section", None, "tensor", None),
            P("dp", "section", None, "tensor", None),
            P("dp", "section", None, "tensor", None),
        ),
        check_vma=False,
    )
```

profile of v0, /device:TPU:0, one launch (start us, length us, event | category | flops | bytes accessed | tf_op | source)
XLA Modules:
  0.0 118.5 jit_solution(13273329882945548308)
XLA Ops:
  8.0 0.0 all-reduce.3.cloned.1.call-start
  8.1 0.7 all-reduce.3.cloned.1.call-update
  8.8 0.0 all-gather.6.cloned.1.call-start
  8.8 0.5 all-gather.6.cloned.1.call-update
  9.3 0.0 all-gather.4.cloned.1.call-start
  9.4 0.2 fusion.16
  9.6 0.1 fusion.17
  9.7 0.1 select_reduce_fusion
  9.9 34.0 %all-reduce.3.cloned.1.call-done = bf16[2,192,768]{2,1,0:T(8,128)(2,1)} async-done(((bf16[2,192,768]{2,1,0:T(8,128)(2,1)}), bf16[2,192,768]{2,1,0:T(8,128)(2,1)}) %all-reduce.3.cloned.1.call-update) | async-done | bytes 589840 | tf_op jit(solution)/shard_map/psum | solution.py:22
  43.9 1.1 convert_element_type.54
  45.1 0.6 gather_fusion
  45.7 2.9 %fusion.12 = (f32[2]{0:T(128)S(1)}, bf16[2,192,768]{2,1,0:T(8,128)(2,1)}) fusion(f32[1,1,2,192,768]{4,3,2,1,0:T(8,128)} %param.11, f32[2]{0:T(128)S(1)} %convert_element_type.55, f32[2,192,768]{2,1,0:T(8,128)S(1)} %gather_fusion, pred[2]{0:T(512)(128)(4,1)S(1)} %compare_and_fusion), kind=kLoop, calls=%fused_computation.24 | loop fusion | flops 3538942 | bytes 2949138 | tf_op jit(solution)/shard_map/reduce_sum | solution.py:48
  48.6 0.0 reduce-scatter.2.cloned.1.call-start
  48.7 1.0 copy-done.1
  49.6 2.3 %convolution_convert_fusion = bf16[2,768,768]{2,1,0:T(8,128)(2,1)} fusion(bf16[2,192,768]{2,1,0:T(8,128)(2,1)S(1)} %copy-done.1), kind=kOutput, calls=%fused_computation.3 | convolution fusion | flops 454164480 | bytes 2949120 | tf_op jit(solution)/shard_map/cki,ckj->cij/dot_general | solution.py:30
  52.0 1.2 %copy-done.3 = f32[1,1,2,192,768]{4,3,2,1,0:T(8,128)S(1)} copy-done((f32[1,1,2,192,768]{4,3,2,1,0:T(8,128)S(1)}, f32[1,1,2,192,768]{4,3,2,1,0:T(8,128)}, u32[]{:S(2)}) %copy-start.3) | copy-done | bytes 1179672
  53.2 1.3 %fusion.5 = f32[1,1,2,192,768]{4,3,2,1,0:T(8,128)} fusion(f32[1,1,2,192,768]{4,3,2,1,0:T(8,128)S(1)} %copy-done.3, f32[2,192,768]{2,1,0:T(8,128)S(1)} %gather_fusion, f32[2]{0:T(128)S(1)} %convert_element_type.55, pred[2]{0:T(512)(128)(4,1)S(1)} %compare_and_fusion), kind=kLoop, calls=%fused_computation.12 | loop fusion | flops 2359296 | bytes 3538954 | tf_op jit(solution)/shard_map/add | solution.py:36
  54.5 18.1 %all-gather.4.cloned.1.call-done = bf16[2,768,768]{2,1,0:T(8,128)(2,1)} async-done(((bf16[2,192,768]{2,1,0:T(8,128)(2,1)}), bf16[2,768,768]{2,1,0:T(8,128)(2,1)}) %all-gather.4.cloned.1.call-update) | async-done | bytes 2359312 | tf_op jit(solution)/shard_map/all_gather | solution.py:27
  72.6 4.6 %multiply_reduce_fusion = (f32[2]{0:T(128)S(1)}, f32[2,192,768]{2,1,0:T(8,128)}) fusion(bf16[1,1,2,768,768]{4,3,2,1,0:T(8,128)(2,1)} %all-gather.6.cloned.1.call-done, bf16[2,768,768]{2,1,0:T(8,128)(2,1)} %all-gather.4.cloned.1.call-done, bf16[1,1,2,192,768]{4,3,2,1,0:T(8,128)(2,1)S(1)} %copy-done), kind=kOutput, calls=%fused_computation.22 | convolution fusion | flops 906854400 | bytes 6488072 | tf_op jit(solution)/shard_map/cik,ckj->cij/dot_general | solution.py:41
  77.3 5.9 %all-reduce = (f32[2]{0:T(128)S(1)}, f32[2]{0:T(128)S(1)}) all-reduce(f32[2]{0:T(128)S(1)} %get-tuple-element.8, f32[2]{0:T(128)S(1)} %get-tuple-element.6), channel_id=1, replica_groups=mesh['dp'=2,'tensor'=4,'section'=4] {'tensor'}, use_global_device_ids=true, to_apply=%region_8.9 | all-reduce | flops 4 | bytes 32 | tf_op jit(solution)/shard_map/psum | solution.py:49
  83.1 2.4 %fusion.13 = bf16[1,1,2,192,768]{4,3,2,1,0:T(8,128)(2,1)} fusion(f32[2,192,768]{2,1,0:T(8,128)} %get-tuple-element.9, f32[2]{0:T(128)S(1)} %rsqrt_multiply_fusion), kind=kLoop, calls=%fused_computation.25 | loop fusion | flops 589824 | bytes 1769480 | tf_op jit(solution)/shard_map/broadcast_in_dim | solution.py:56
  85.5 2.0 %fusion.3 = f32[1,1,2,192,768]{4,3,2,1,0:T(8,128)} fusion(bf16[2,192,768]{2,1,0:T(8,128)(2,1)S(1)} %copy-done.1, bf16[2,768,768]{2,1,0:T(8,128)(2,1)S(1)} %copy-done.2, f32[1,1,2,192,768]{4,3,2,1,0:T(8,128)S(1)} %copy-done.4), kind=kOutput, calls=%fused_computation.9 | convolution fusion | flops 453869568 | bytes 5308416 | tf_op jit(solution)/shard_map/cik,cjk->cij/dot_general | solution.py:28
  87.5 20.7 %reduce-scatter.2.cloned.1.call-done = bf16[2,192,768]{2,1,0:T(8,128)(2,1)} async-done(((bf16[2,768,768]{2,1,0:T(8,128)(2,1)}), bf16[2,192,768]{2,1,0:T(8,128)(2,1)}) %reduce-scatter.2.cloned.1.call-update) | async-done | bytes 589840 | tf_op jit(solution)/shard_map/reduce_scatter | solution.py:31
  108.2 2.6 %fusion.11 = f32[1,1,2,192,768]{4,3,2,1,0:T(8,128)} fusion(bf16[2,192,768]{2,1,0:T(8,128)(2,1)} %reduce-scatter.2.cloned.1.call-done, f32[1,1,2,192,768]{4,3,2,1,0:T(8,128)} %param.10), kind=kLoop, calls=%fused_computation.20 | loop fusion | flops 1179648 | bytes 2949120 | tf_op jit(solution)/shard_map/broadcast_in_dim | solution.py:54
  (19 shorter events, 0.1 us)
Async XLA Ops:
  8.0 64.6 %copy-start = (bf16[1,1,2,192,768]{4,3,2,1,0:T(8,128)(2,1)S(1)}, bf16[1,1,2,192,768]{4,3,2,1,0:T(8,128)(2,1)}, u32[]{:S(2)}) copy-start(bf16[1,1,2,192,768]{4,3,2,1,0:T(8,128)(2,1)} %param.12) | copy-start | bytes 1769476
  8.0 1.4 %copy-start.5 = (s32[2,1]{0,1:T(1,128)S(1)}, s32[2,1]{0,1:T(1,128)}, u32[]{:S(2)}) copy-start(s32[2,1]{0,1:T(1,128)} %param.8) | copy-start | bytes 28
  8.0 35.9 %all-reduce.3.cloned.1.call-start = ((), (), s32[]{:S(2)}) async-start(), calls=%async_computation.1 | async-start | bytes 1179648 | tf_op jit(solution)/shard_map/psum | solution.py:22
  8.8 45.8 %all-gather.6.cloned.1.call-start = ((), (), s32[]{:S(2)}) async-start(), calls=%async_computation.4 | async-start | bytes 2949120 | tf_op jit(solution)/shard_map/all_gather | solution.py:44
  9.3 63.3 %all-gather.4.cloned.1.call-start = ((), (), s32[]{:S(2)}) async-start(), calls=%async_computation.2 | async-start | bytes 2949120 | tf_op jit(solution)/shard_map/all_gather | solution.py:27
  48.6 1.1 copy-start.1
  48.6 59.6 %reduce-scatter.2.cloned.1.call-start = ((), (), s32[]{:S(2)}) async-start(), calls=%async_computation.3 | async-start | bytes 2949120 | tf_op jit(solution)/shard_map/reduce_scatter | solution.py:31
  51.9 1.3 %copy-start.3 = (f32[1,1,2,192,768]{4,3,2,1,0:T(8,128)S(1)}, f32[1,1,2,192,768]{4,3,2,1,0:T(8,128)}, u32[]{:S(2)}) copy-start(f32[1,1,2,192,768]{4,3,2,1,0:T(8,128)} %param.11) | copy-start | bytes 3538948
  72.6 12.9 %copy-start.2 = (bf16[2,768,768]{2,1,0:T(8,128)(2,1)S(1)}, bf16[2,768,768]{2,1,0:T(8,128)(2,1)}, u32[]{:S(2)}) copy-start(bf16[2,768,768]{2,1,0:T(8,128)(2,1)} %all-gather.4.cloned.1.call-done) | copy-start | bytes 7077892
  83.1 2.4 %copy-start.4 = (f32[1,1,2,192,768]{4,3,2,1,0:T(8,128)S(1)}, f32[1,1,2,192,768]{4,3,2,1,0:T(8,128)}, u32[]{:S(2)}) copy-start(f32[1,1,2,192,768]{4,3,2,1,0:T(8,128)} %param.9) | copy-start | bytes 3538948
Sparse Core Ops, SparseCore 0:
  11.2 32.7 all-reduce.2
Sparse Core Ops, SparseCore 1:
  10.9 26.6 all-gather.5
  48.7 23.9 all-gather.3
  75.2 33.0 reduce-scatter.1
where the time goes:
time: 119 us; the launch traced here: 118 us
  waiting for transfers between devices  74.1 us (62%)
  between operations  15.7 us (13%)
  other arithmetic  10.8 us (9%)
  matrix products  8.91 us (7%)
  blocking collectives  5.86 us (5%)
  local copies, waits for them, and re-layouts  2.88 us (2%)
    psum x1, waiting for transfers between devices, per_device(): lax.psum(local_grads.astype(jnp.float32).astype(jnp.bfloat16), 'dp')  34 us
    reduce_scatter x1, waiting for transfers between devices, per_device(): lax.psum_scatter(partials.astype(jnp.bfloat16), 'tensor', scatter_dimensi...  20.7 us
    all_gather x1, waiting for transfers between devices, per_device(): gathered = lax.all_gather(gradient, 'tensor', axis=1, tiled=True)  18.1 us
    psum x1, blocking collectives, per_device(): precond_sq, adam_sq = lax.psum((precond_sq, adam_sq), 'tensor')  5.86 us
    dot_general x1, matrix products, per_device(): jnp.einsum('cik,ckj->cij', mixed, lax.all_gather(right_root[0, 0], 'tenso...  4.63 us
    reduce_sum x1, other arithmetic, per_device(): adam_sq = jnp.sum(adam_dir * adam_dir, axis=(1, 2))  2.89 us
    broadcast_in_dim x1, other arithmetic, per_device(): right_new[None, None]  2.65 us
    broadcast_in_dim x1, other arithmetic, per_device(): direction[None, None]  2.39 us
  transfers between devices with their start and end apart: 4, of which 3 were waited for; matrix products, arithmetic and copies ran while one was open for 15% of the time, Pallas kernels for 0%

commit v1 on v0

--- a/solution.py
+++ b/solution.py
@@ -1,12 +1,20 @@
+import functools
+
 import jax
 import jax.numpy as jnp
 from jax import lax
+from jax.experimental import pallas as pl
+from jax.experimental.pallas import tpu as pltpu
 from jax.sharding import PartitionSpec as P
 
 CAP = 2
-
-
-def per_device(grads, owner, left_stat, right_stat, second_moment, left_root, right_root):
+MESH = pl.DeviceIdType.MESH
+
+X1, X2, X3, Y1, Y2, B1, B2, B3, B4, B5, B6 = range(0, 22, 2)
+Z = 22
+
+
+def plain_step(grads, owner, left_stat, right_stat, second_moment, left_root, right_root):
     block_count = owner.shape[0]
     my_rank = lax.axis_index("dp")
     owners_list = owner[:, 0]
@@ -57,25 +65,293 @@
     )
 
 
+def fold(values):
+    rows, columns = values.shape
+    total = jnp.sum(values.reshape(rows // 8, 8, columns), axis=0)
+    total = sum(total[:, i : i + 128] for i in range(0, columns, 128))
+    return jnp.sum(total, axis=0, keepdims=True)
+
+
+def kernel(
+    owner, grads, left_stat, right_stat, second, left_root, right_root,
+    left_out, right_out, second_out, direction_out,
+    mine, theirs, summed, gradient, root_all, root_left, left_buf, right_buf, second_buf,
+    mixed, precond, direction, turned, norms, local_sem, out_sem, send_sem, recv_sem,
+):
+    d, t = lax.axis_index("dp"), lax.axis_index("tensor")
+    blocks, rows, width = mine.shape
+    half, tile = rows // 2, 256
+    tiles = width // tile
+    other = 1 - d
+    sibling, across, far = t + 1 - 2 * (t % 2), (t + 2) % 4, 3 - t
+    peer_x, peer_s, peer_y = {"dp": other}, {"tensor": sibling}, {"tensor": across}
+    peer_f = {"tensor": far}
+
+    def load(k, source, target):
+        return pltpu.make_async_copy(source, target, local_sem.at[k])
+
+    def place(rank, r):
+        return pl.ds(pl.multiple_of(rank * rows + r * half, 16), half)
+
+    def whole(rank):
+        return pl.ds(pl.multiple_of(rank * rows, 16), rows)
+
+    def send(k, source, target, device):
+        return pltpu.make_async_remote_copy(
+            src_ref=source, dst_ref=target, send_sem=send_sem.at[k], recv_sem=recv_sem.at[k],
+            device_id=device, device_id_type=MESH,
+        )
+
+    def go(k, source, target, device):
+        copy = send(k, source, target, device)
+        copy.start()
+        sent.append(copy)
+
+    def arrived(k, target, device):
+        send(k, target, target, device).wait_recv()
+
+    sent = []
+    norms[t] = jnp.zeros((8, 128), jnp.float32)
+    loads = [
+        load(0, grads, mine),
+        load(1, right_root, root_all.at[:, whole(t)]),
+        load(2, second, second_buf),
+        load(3, left_root, root_left),
+        load(4, left_stat, left_buf),
+        load(5, right_stat, right_buf),
+    ]
+    for copy in loads:
+        copy.start()
+
+    barrier = pltpu.get_barrier_semaphore()
+    for peer in (peer_x, peer_s, peer_y, peer_f):
+        pl.semaphore_signal(barrier, inc=1, device_id=peer, device_id_type=MESH)
+    pl.semaphore_wait(barrier, 4)
+
+    for r in range(2):
+        part = pl.ds(r * half, half)
+        go(X1 + r, grads.at[other, part], theirs.at[other, part], peer_x)
+    go(Y2, right_root.at[0], root_all.at[0, whole(t)], peer_y)
+    for r in range(2):
+        part = pl.ds(r * half, half)
+        go(X2 + r, grads.at[d, part], theirs.at[d, part], peer_x)
+    for c in range(2):
+        go(B5 + c, right_root.at[c], root_all.at[c, whole(t)], peer_s)
+
+    def add(block, r):
+        def body(i, carry):
+            at = pl.ds(pl.multiple_of(r * half + i * 16, 16), 16)
+            to = pl.ds(pl.multiple_of(t * rows + r * half + i * 16, 16), 16)
+            total = mine[block, at].astype(jnp.float32) + theirs[block, at].astype(jnp.float32)
+            summed[block, to] = total.astype(jnp.bfloat16)
+            return carry
+
+        lax.fori_loop(0, half // 16, body, 0, unroll=2)
+
+    owners = [owner[b, 0] for b in range(blocks)]
+    weights = []
+    for c in range(CAP):
+        row = []
+        for b in range(blocks):
+            if b < c:
+                row.append(None)
+                continue
+            rank = sum(((owners[e] == owners[b]).astype(jnp.int32) for e in range(b)), jnp.int32(0))
+            row.append(((owners[b] == d) & (rank == c)).astype(jnp.float32))
+        weights.append(row)
+
+    def select(first, count):
+        def body(i, carry):
+            at = pl.ds(pl.multiple_of(first + i * 16, 16), 16)
+            terms = [summed[b, at].astype(jnp.float32) for b in range(blocks)]
+            for c in range(CAP):
+                total = sum(terms[b] * weights[c][b] for b in range(c, blocks))
+                gradient[c, at] = total.astype(jnp.bfloat16)
+            return carry
+
+        lax.fori_loop(0, count // 16, body, 0, unroll=2)
+
+    loads[0].wait()
+    for r in range(2):
+        arrived(X1 + r, theirs.at[d, pl.ds(r * half, half)], peer_x)
+        add(d, r)
+        go(Y1 + r, summed.at[d, place(t, r)], summed.at[d, place(t, r)], peer_y)
+        go(B1 + r, summed.at[d, place(t, r)], summed.at[d, place(t, r)], peer_s)
+    go(Y2 + 1, right_root.at[1], root_all.at[1, whole(t)], peer_y)
+    for r in range(2):
+        arrived(X2 + r, theirs.at[other, pl.ds(r * half, half)], peer_x)
+        add(other, r)
+        go(B2 + r, summed.at[other, place(t, r)], summed.at[other, place(t, r)], peer_s)
+        arrived(Y1 + r, summed.at[d, place(across, r)], peer_y)
+        go(X3 + r, summed.at[d, place(across, r)], summed.at[d, place(across, r)], peer_x)
+        go(B3 + r, summed.at[d, place(across, r)], summed.at[d, place(across, r)], peer_s)
+    arrived(Y2, root_all.at[0, whole(across)], peer_y)
+    go(B6, root_all.at[0, whole(across)], root_all.at[0, whole(across)], peer_s)
+
+    select(t * rows, rows)
+    loads[2].wait()
+    for c in range(CAP):
+
+        def moment(i, total):
+            at = pl.ds(pl.multiple_of(i * 16, 16), 16)
+            g = gradient[c, pl.ds(pl.multiple_of(t * rows + i * 16, 16), 16)].astype(jnp.float32)
+            new = 0.9 * second_buf[c, at] + 0.1 * g * g
+            second_buf[c, at] = new
+            adam = g / (jnp.sqrt(new) + 1e-08)
+            return total + fold(adam * adam)
+
+        norms[t, c : c + 1] = lax.fori_loop(
+            0, rows // 16, moment, jnp.zeros((1, 128), jnp.float32)
+        )
+    stores = [pltpu.make_async_copy(second_buf, second_out, out_sem.at[0])]
+    stores[0].start()
+
+    for r in range(2):
+        arrived(B1 + r, summed.at[d, place(sibling, r)], peer_s)
+        arrived(B2 + r, summed.at[other, place(sibling, r)], peer_s)
+    select(sibling * rows, rows)
+    for r in range(2):
+        arrived(X3 + r, summed.at[other, place(across, r)], peer_x)
+        go(B4 + r, summed.at[other, place(across, r)], summed.at[other, place(across, r)], peer_s)
+        select(across * rows + r * half, half)
+    arrived(Y2 + 1, root_all.at[1, whole(across)], peer_y)
+    go(B6 + 1, root_all.at[1, whole(across)], root_all.at[1, whole(across)], peer_s)
+    for r in range(2):
+        arrived(B3 + r, summed.at[d, place(far, r)], peer_s)
+        arrived(B4 + r, summed.at[other, place(far, r)], peer_s)
+        select(far * rows + r * half, half)
+    loads[3].wait()
+
+    def tiled(body):
+        def step(i, carry):
+            body(i // tiles, pl.ds(pl.multiple_of((i % tiles) * tile, tile), tile))
+            return carry
+
+        lax.fori_loop(0, CAP * tiles, step, 0)
+
+    def mix(c, cut):
+        mixed[c, :, cut] = jnp.dot(
+            root_left[c], gradient[c, :, cut], preferred_element_type=jnp.float32
+        ).astype(jnp.bfloat16)
+
+    tiled(mix)
+    loads[1].wait()
+    for c in range(2):
+        arrived(B5 + c, root_all.at[c, whole(sibling)], peer_s)
+        arrived(B6 + c, root_all.at[c, whole(far)], peer_s)
+    for c in range(CAP):
+
+        def multiply(i, total):
+            cut = pl.ds(pl.multiple_of(i * tile, tile), tile)
+            product = jnp.dot(mixed[c], root_all[c, :, cut], preferred_element_type=jnp.float32)
+            precond[c, :, cut] = product
+            return total + fold(product * product)
+
+        norms[t, CAP + c : CAP + c + 1] = lax.fori_loop(
+            0, tiles, multiply, jnp.zeros((1, 128), jnp.float32)
+        )
+    for k, peer in enumerate((peer_s, peer_y, peer_f)):
+        go(Z + k, norms.at[t], norms.at[t], peer)
+
+    loads[4].wait()
+
+    def left(c, cut):
+        product = lax.dot_general(
+            gradient[c, whole(t)], gradient[c, cut], (((1,), (1,)), ((), ())),
+            preferred_element_type=jnp.float32,
+        )
+        left_buf[c, :, cut] = 0.95 * left_buf[c, :, cut] + 0.05 * product
+
+    tiled(left)
+    stores.append(pltpu.make_async_copy(left_buf, left_out, out_sem.at[1]))
+    stores[1].start()
+    loads[5].wait()
+    window = pl.ds(pl.multiple_of(128 * ((3 * t) // 2), 128), tile)
+    shift = pl.ds(pl.multiple_of(64 * (t % 2), 64), rows)
+    for c in range(CAP):
+        turned[c] = gradient[c, :, window].T
+
+    def right(c, cut):
+        product = jnp.dot(
+            turned[c, shift], gradient[c, :, cut], preferred_element_type=jnp.float32
+        )
+        right_buf[c, :, cut] = 0.95 * right_buf[c, :, cut] + 0.05 * product
+
+    tiled(right)
+    stores.append(pltpu.make_async_copy(right_buf, right_out, out_sem.at[2]))
+    stores[2].start()
+
+    for k, (rank, peer) in enumerate(((sibling, peer_s), (across, peer_y), (far, peer_f))):
+        arrived(Z + k, norms.at[rank], peer)
+    total = jnp.sum(norms[0] + norms[1] + norms[2] + norms[3], axis=1, keepdims=True)
+    for c in range(CAP):
+        scaling = jnp.sqrt(total[c : c + 1]) / jnp.sqrt(total[CAP + c : CAP + c + 1] + 1e-06)
+
+        def scale(i, carry):
+            at = pl.ds(pl.multiple_of(i * 16, 16), 16)
+            direction[c, at] = (precond[c, at] * scaling).astype(jnp.bfloat16)
+            return carry
+
+        lax.fori_loop(0, rows // 16, scale, 0, unroll=2)
+    stores.append(pltpu.make_async_copy(direction, direction_out, out_sem.at[3]))
+    stores[3].start()
+    for copy in sent:
+        copy.wait_send()
+    for copy in stores:
+        copy.wait()
+
+
+def fused_step(grads, owner, left_stat, right_stat, second_moment, left_root, right_root):
+    _, blocks, rows, width = grads.shape
+    full = (CAP, width, width)
+    part = (CAP, rows, width)
+    f32, bf16 = jnp.float32, jnp.bfloat16
+    anywhere = pl.BlockSpec(memory_space=pl.ANY)
+    outs = pl.pallas_call(
+        kernel,
+        out_shape=[jax.ShapeDtypeStruct(part, f32)] * 3 + [jax.ShapeDtypeStruct(part, bf16)],
+        in_specs=[pl.BlockSpec(memory_space=pltpu.SMEM)] + [anywhere] * 6,
+        out_specs=[anywhere] * 4,
+        scratch_shapes=[
+            pltpu.VMEM((blocks, rows, width), bf16),
+            pltpu.VMEM((blocks, rows, width), bf16),
+            pltpu.VMEM((blocks, width, width), bf16),
+            pltpu.VMEM(full, bf16),
+            pltpu.VMEM(full, bf16),
+            pltpu.VMEM(part, bf16),
+            pltpu.VMEM(part, f32),
+            pltpu.VMEM(part, f32),
+            pltpu.VMEM(part, f32),
+            pltpu.VMEM(part, bf16),
+            pltpu.VMEM(part, f32),
+            pltpu.VMEM(part, bf16),
+            pltpu.VMEM((CAP, 256, width), bf16),
+            pltpu.VMEM((4, 8, 128), f32),
+            pltpu.SemaphoreType.DMA((6,)),
+            pltpu.SemaphoreType.DMA((4,)),
+            pltpu.SemaphoreType.DMA((Z + 3,)),
+            pltpu.SemaphoreType.DMA((Z + 3,)),
+        ],
+        compiler_params=pltpu.CompilerParams(
+            collective_id=0, has_side_effects=True, vmem_limit_bytes=48 * 1024 * 1024
+        ),
+    )(
+        owner, grads[0], left_stat[0, 0], right_stat[0, 0], second_moment[0, 0],
+        left_root[0, 0], right_root[0, 0],
+    )
+    return tuple(out[None, None] for out in outs)
+
+
 def solution(mesh):
-    placed = (
-        P("dp", "section", "tensor", None),
-        P("section", None),
-        P("dp", "section", None, "tensor", None),
-        P("dp", "section", None, "tensor", None),
-        P("dp", "section", None, "tensor", None),
-        P("dp", "section", None, "tensor", None),
-        P("dp", "section", None, "tensor", None),
-    )
+    state = P("dp", "section", None, "tensor", None)
+    placed = (P("dp", "section", "tensor", None), P("section", None)) + (state,) * 5
+
+    def step(*args):
+        _, blocks, rows, width = args[0].shape
+        fits = mesh.shape["dp"] == 2 and mesh.shape["tensor"] == 4 and blocks == 2
+        fits = fits and rows == 192 and width == 768 and args[2].shape[2] == CAP
+        return (fused_step if fits else plain_step)(*args)
+
     return jax.shard_map(
-        per_device,
-        mesh=mesh,
-        in_specs=placed,
-        out_specs=(
-            P("dp", "section", None, "tensor", None),
-            P("dp", "section", None, "tensor", None),
-            P("dp", "section", None, "tensor", None),
-            P("dp", "section", None, "tensor", None),
-        ),
-        check_vma=False,
-    )
+        step, mesh=mesh, in_specs=placed, out_specs=(state,) * 4, check_vma=False
+    )

time: 119 us -> 43.8 us (0.37)
  waiting for transfers between devices: 74.1 us -> 0 us
  Pallas kernels: 0 us -> 34.7 us
  between operations: 15.7 us -> 0.64 us
  other arithmetic: 10.8 us -> 0 us
  matrix products: 8.91 us -> 0 us
  blocking collectives: 5.86 us -> 0 us
  local copies, waits for them, and re-layouts: 2.88 us -> 7.79 us
    pallas_call x0 -> x1, Pallas kernels: none -> 34.7 us  [fused_step(): pl.pallas_call(kernel, out_shape=[jax.ShapeDtypeStruct(part, f32)] * 3 +...]
    psum x1 -> x0, waiting for transfers between devices: 34 us -> none  [per_device(): lax.psum(local_grads.astype(jnp.float32).astype(jnp.bfloat16), 'dp')]
    reduce_scatter x1 -> x0, waiting for transfers between devices: 20.7 us -> none  [per_device(): lax.psum_scatter(partials.astype(jnp.bfloat16), 'tensor', scatter_dimensi...]
    all_gather x2 -> x0, waiting for transfers between devices: 18.1 us -> none  [the longest x1 18.1 us: per_device(): gathered = lax.all_gather(gradient, 'tensor', axis=1, tiled=True)]
    dot_general x3 -> x0, matrix products: 8.91 us -> none  [the longest x1 4.63 us: per_device(): jnp.einsum('cik,ckj->cij', mixed, lax.all_gather(right_root[0, 0], 'tenso...]
    psum x1 -> x0, blocking collectives: 5.86 us -> none  [per_device(): precond_sq, adam_sq = lax.psum((precond_sq, adam_sq), 'tensor')]
    unnamed x12 -> x11, local copies, waits for them, and re-layouts: 2.25 us -> 7.79 us
    broadcast_in_dim x2 -> x0, other arithmetic: 5.04 us -> none  [the longest x1 2.65 us: per_device(): right_new[None, None]]
  transfers between devices with their start and end apart: 4 -> 0, of which waited for: 3 -> 0; matrix products, arithmetic and copies ran while one was open for 15% -> 0% of each run, Pallas kernels for 0% -> 0%
where the time goes in v1:
time: 43.8 us; the launch traced here: 43.1 us
  Pallas kernels  34.7 us (79%)
  local copies, waits for them, and re-layouts  7.79 us (18%)
  between operations  0.64 us (1%)
    pallas_call x1, Pallas kernels, fused_step(): pl.pallas_call(kernel, out_shape=[jax.ShapeDtypeStruct(part, f32)] * 3 +...  34.7 us
    unnamed x11, local copies, waits for them, and re-layouts  7.79 us

profile of v1, /device:TPU:0, one launch (start us, length us, event | category | flops | bytes accessed | tf_op | source)
XLA Modules:
  0.0 43.1 jit_solution(9523898215523297061)
XLA Ops:
  0.6 0.7 %copy.11.owner = s32[2,1]{1,0:T(2,128)S(1)} copy(s32[2,1]{0,1:T(1,128)} %param.8) | data formatting | bytes 16 | tf_op args[1]
  1.4 0.0 copy-start
  1.4 1.1 %copy-done = bf16[1,2,192,768]{3,2,1,0:T(8,128)(2,1)S(1)} copy-done((bf16[1,2,192,768]{3,2,1,0:T(8,128)(2,1)S(1)}, bf16[1,2,192,768]{3,2,1,0:T(8,128)(2,1)}, u32[]{:S(2)}) %copy-start) | copy-done | bytes 589848
  2.4 0.0 copy-start.1
  2.4 1.1 %copy-done.1 = bf16[1,1,2,192,768]{4,3,2,1,0:T(8,128)(2,1)S(1)} copy-done((bf16[1,1,2,192,768]{4,3,2,1,0:T(8,128)(2,1)S(1)}, bf16[1,1,2,192,768]{4,3,2,1,0:T(8,128)(2,1)}, u32[]{:S(2)}) %copy-start.1) | copy-done | bytes 589848
  3.5 0.0 copy-start.2
  3.5 1.1 %copy-done.2 = bf16[1,1,2,192,768]{4,3,2,1,0:T(8,128)(2,1)S(1)} copy-done((bf16[1,1,2,192,768]{4,3,2,1,0:T(8,128)(2,1)S(1)}, bf16[1,1,2,192,768]{4,3,2,1,0:T(8,128)(2,1)}, u32[]{:S(2)}) %copy-start.2) | copy-done | bytes 589848
  4.6 34.7 %shard_map.102 = (f32[2,192,768]{2,1,0:T(8,128)S(1)}, f32[2,192,768]{2,1,0:T(8,128)S(1)}, f32[2,192,768]{2,1,0:T(8,128)S(1)}, bf16[2,192,768]{2,1,0:T(8,128)(2,1)S(1)}) custom-call(s32[2,1]{1,0:T(2,128)S(1)} %copy.11.owner, bf16[2,192,768]{2,1,0:T(8,128)(2,1)S(1)} %bitcast.14, f32[2,192,768]{2,1,0:T(8,128)} %bitcast.17, f32[2,192,768]{2,1,0:T(8,128)} %bitcast.18, ...), custom_call_target="tpu_custom_call" | custom-call | tf_op jit(solution)/shard_map/pallas_call | solution.py:310
  39.3 1.0 %copy.16 = f32[1,1,2,192,768]{4,3,2,1,0:T(8,128)} copy(f32[1,1,2,192,768]{4,3,2,1,0:T(8,128)S(1)} %bitcast.12) | data formatting | bytes 2359296
  40.3 1.0 %copy.17 = f32[1,1,2,192,768]{4,3,2,1,0:T(8,128)} copy(f32[1,1,2,192,768]{4,3,2,1,0:T(8,128)S(1)} %bitcast.11) | data formatting | bytes 2359296
  41.3 1.0 %copy.18 = f32[1,1,2,192,768]{4,3,2,1,0:T(8,128)} copy(f32[1,1,2,192,768]{4,3,2,1,0:T(8,128)S(1)} %bitcast.10) | data formatting | bytes 2359296
  42.3 0.8 %copy.19 = bf16[1,1,2,192,768]{4,3,2,1,0:T(8,128)(2,1)} copy(bf16[1,1,2,192,768]{4,3,2,1,0:T(8,128)(2,1)S(1)} %bitcast.13) | data formatting | bytes 1179648
Async XLA Ops:
  1.4 1.1 %copy-start = (bf16[1,2,192,768]{3,2,1,0:T(8,128)(2,1)S(1)}, bf16[1,2,192,768]{3,2,1,0:T(8,128)(2,1)}, u32[]{:S(2)}) copy-start(bf16[1,2,192,768]{3,2,1,0:T(8,128)(2,1)} %param.7) | copy-start | bytes 1769476
  2.4 1.1 %copy-start.1 = (bf16[1,1,2,192,768]{4,3,2,1,0:T(8,128)(2,1)S(1)}, bf16[1,1,2,192,768]{4,3,2,1,0:T(8,128)(2,1)}, u32[]{:S(2)}) copy-start(bf16[1,1,2,192,768]{4,3,2,1,0:T(8,128)(2,1)} %param.12) | copy-start | bytes 1769476
  3.5 1.1 %copy-start.2 = (bf16[1,1,2,192,768]{4,3,2,1,0:T(8,128)(2,1)S(1)}, bf16[1,1,2,192,768]{4,3,2,1,0:T(8,128)(2,1)}, u32[]{:S(2)}) copy-start(bf16[1,1,2,192,768]{4,3,2,1,0:T(8,128)(2,1)} %param.13) | copy-start | bytes 1769476

commit v2 on v1

--- a/solution.py
+++ b/solution.py
@@ -10,8 +10,8 @@
 CAP = 2
 MESH = pl.DeviceIdType.MESH
 
-X1, X2, X3, Y1, Y2, B1, B2, B3, B4, B5, B6 = range(0, 22, 2)
-Z = 22
+CHUNKS = 4
+X1, X2, X3, Y1, Y2, B1, B2, B3, B4, B5, B6, Z = range(0, 12 * CHUNKS, CHUNKS)
 
 
 def plain_step(grads, owner, left_stat, right_stat, second_moment, left_root, right_root):
@@ -74,13 +74,13 @@
 
 def kernel(
     owner, grads, left_stat, right_stat, second, left_root, right_root,
-    left_out, right_out, second_out, direction_out,
-    mine, theirs, summed, gradient, root_all, root_left, left_buf, right_buf, second_buf,
-    mixed, precond, direction, turned, norms, local_sem, out_sem, send_sem, recv_sem,
+    left_out, right_out, second_out, precond, totals,
+    mine, theirs, summed, gradient, root_all, root_left,
+    mixed, turned, norms, local_sem, send_sem, recv_sem,
 ):
     d, t = lax.axis_index("dp"), lax.axis_index("tensor")
     blocks, rows, width = mine.shape
-    half, tile = rows // 2, 256
+    chunk, half, tile = rows // CHUNKS, rows // 2, 256
     tiles = width // tile
     other = 1 - d
     sibling, across, far = t + 1 - 2 * (t % 2), (t + 2) % 4, 3 - t
@@ -91,10 +91,13 @@
         return pltpu.make_async_copy(source, target, local_sem.at[k])
 
     def place(rank, r):
-        return pl.ds(pl.multiple_of(rank * rows + r * half, 16), half)
+        return pl.ds(pl.multiple_of(rank * rows + r * chunk, 16), chunk)
 
     def whole(rank):
         return pl.ds(pl.multiple_of(rank * rows, 16), rows)
+
+    def root_part(rank, k):
+        return root_all.at[k // 2, pl.ds(pl.multiple_of(rank * rows + k % 2 * half, 16), half)]
 
     def send(k, source, target, device):
         return pltpu.make_async_remote_copy(
@@ -109,46 +112,58 @@
 
     def arrived(k, target, device):
         send(k, target, target, device).wait_recv()
+
+    def go_rows(k, block, at, device):
+        go(k, summed.at[block, at], summed.at[block, at], device)
+
+    def go_x(k):
+        block, part = (other, d)[k // CHUNKS], pl.ds(k % CHUNKS * chunk, chunk)
+        go(X1 + k, grads.at[block, part], theirs.at[block, part], peer_x)
+
+    def go_root(k):
+        source = right_root.at[k // 2, pl.ds(k % 2 * half, half)]
+        go(Y2 + k, source, root_part(t, k), peer_y)
+
+    def root_came(k):
+        arrived(Y2 + k, root_part(across, k), peer_y)
+        go(B6 + k, root_part(across, k), root_part(across, k), peer_s)
 
     sent = []
     norms[t] = jnp.zeros((8, 128), jnp.float32)
     loads = [
         load(0, grads, mine),
         load(1, right_root, root_all.at[:, whole(t)]),
-        load(2, second, second_buf),
+        load(2, second, second_out),
         load(3, left_root, root_left),
-        load(4, left_stat, left_buf),
-        load(5, right_stat, right_buf),
+        load(4, left_stat, left_out),
+        load(5, right_stat, right_out),
     ]
-    for copy in loads:
-        copy.start()
+    loads[0].start()
 
     barrier = pltpu.get_barrier_semaphore()
     for peer in (peer_x, peer_s, peer_y, peer_f):
         pl.semaphore_signal(barrier, inc=1, device_id=peer, device_id_type=MESH)
     pl.semaphore_wait(barrier, 4)
 
-    for r in range(2):
-        part = pl.ds(r * half, half)
-        go(X1 + r, grads.at[other, part], theirs.at[other, part], peer_x)
-    go(Y2, right_root.at[0], root_all.at[0, whole(t)], peer_y)
-    for r in range(2):
-        part = pl.ds(r * half, half)
-        go(X2 + r, grads.at[d, part], theirs.at[d, part], peer_x)
+    go_x(0)
+    go_root(0)
+    go_x(1)
+    for copy in loads[1:]:
+        copy.start()
     for c in range(2):
         go(B5 + c, right_root.at[c], root_all.at[c, whole(t)], peer_s)
 
     def add(block, r):
         def body(i, carry):
-            at = pl.ds(pl.multiple_of(r * half + i * 16, 16), 16)
-            to = pl.ds(pl.multiple_of(t * rows + r * half + i * 16, 16), 16)
+            at = pl.ds(pl.multiple_of(r * chunk + i * 16, 16), 16)
+            to = pl.ds(pl.multiple_of(t * rows + r * chunk + i * 16, 16), 16)
             total = mine[block, at].astype(jnp.float32) + theirs[block, at].astype(jnp.float32)
             summed[block, to] = total.astype(jnp.bfloat16)
             return carry
 
-        lax.fori_loop(0, half // 16, body, 0, unroll=2)
-
-    owners = [owner[b, 0] for b in range(blocks)]
+        lax.fori_loop(0, chunk // 16, body, 0)
+
+    owners = [owner[b] for b in range(blocks)]
     weights = []
     for c in range(CAP):
         row = []
@@ -169,24 +184,35 @@
                 gradient[c, at] = total.astype(jnp.bfloat16)
             return carry
 
-        lax.fori_loop(0, count // 16, body, 0, unroll=2)
+        lax.fori_loop(0, count // 16, body, 0)
+
+    def across_came(r):
+        arrived(Y1 + r, summed.at[d, place(across, r)], peer_y)
+        go_rows(X3 + r, d, place(across, r), peer_x)
+        go_rows(B3 + r, d, place(across, r), peer_s)
 
     loads[0].wait()
-    for r in range(2):
-        arrived(X1 + r, theirs.at[d, pl.ds(r * half, half)], peer_x)
+    for r in range(CHUNKS):
+        arrived(X1 + r, theirs.at[d, pl.ds(r * chunk, chunk)], peer_x)
+        go_x(2 + r)
         add(d, r)
-        go(Y1 + r, summed.at[d, place(t, r)], summed.at[d, place(t, r)], peer_y)
-        go(B1 + r, summed.at[d, place(t, r)], summed.at[d, place(t, r)], peer_s)
-    go(Y2 + 1, right_root.at[1], root_all.at[1, whole(t)], peer_y)
-    for r in range(2):
-        arrived(X2 + r, theirs.at[other, pl.ds(r * half, half)], peer_x)
+        go_rows(Y1 + r, d, place(t, r), peer_y)
+        go_rows(B1 + r, d, place(t, r), peer_s)
+        if r >= 2:
+            across_came(r - 2)
+    go_root(1)
+    go_root(2)
+    for r in range(CHUNKS):
+        arrived(X2 + r, theirs.at[other, pl.ds(r * chunk, chunk)], peer_x)
+        if 2 + CHUNKS + r < 2 * CHUNKS:
+            go_x(2 + CHUNKS + r)
         add(other, r)
-        go(B2 + r, summed.at[other, place(t, r)], summed.at[other, place(t, r)], peer_s)
-        arrived(Y1 + r, summed.at[d, place(across, r)], peer_y)
-        go(X3 + r, summed.at[d, place(across, r)], summed.at[d, place(across, r)], peer_x)
-        go(B3 + r, summed.at[d, place(across, r)], summed.at[d, place(across, r)], peer_s)
-    arrived(Y2, root_all.at[0, whole(across)], peer_y)
-    go(B6, root_all.at[0, whole(across)], root_all.at[0, whole(across)], peer_s)
+        go_rows(B2 + r, other, place(t, r), peer_s)
+        if r + CHUNKS - 2 < CHUNKS:
+            across_came(r + CHUNKS - 2)
+    root_came(0)
+    root_came(1)
+    go_root(3)
 
     select(t * rows, rows)
     loads[2].wait()
@@ -195,31 +221,31 @@
         def moment(i, total):
             at = pl.ds(pl.multiple_of(i * 16, 16), 16)
             g = gradient[c, pl.ds(pl.multiple_of(t * rows + i * 16, 16), 16)].astype(jnp.float32)
-            new = 0.9 * second_buf[c, at] + 0.1 * g * g
-            second_buf[c, at] = new
+            new = 0.9 * second_out[c, at] + 0.1 * g * g
+            second_out[c, at] = new
             adam = g / (jnp.sqrt(new) + 1e-08)
             return total + fold(adam * adam)
 
         norms[t, c : c + 1] = lax.fori_loop(
             0, rows // 16, moment, jnp.zeros((1, 128), jnp.float32)
         )
-    stores = [pltpu.make_async_copy(second_buf, second_out, out_sem.at[0])]
-    stores[0].start()
-
-    for r in range(2):
-        arrived(B1 + r, summed.at[d, place(sibling, r)], peer_s)
-        arrived(B2 + r, summed.at[other, place(sibling, r)], peer_s)
-    select(sibling * rows, rows)
-    for r in range(2):
+
+    for r in range(CHUNKS):
         arrived(X3 + r, summed.at[other, place(across, r)], peer_x)
-        go(B4 + r, summed.at[other, place(across, r)], summed.at[other, place(across, r)], peer_s)
-        select(across * rows + r * half, half)
-    arrived(Y2 + 1, root_all.at[1, whole(across)], peer_y)
-    go(B6 + 1, root_all.at[1, whole(across)], root_all.at[1, whole(across)], peer_s)
-    for r in range(2):
+        go_rows(B4 + r, other, place(across, r), peer_s)
+        if r == 0:
+            for k in range(CHUNKS):
+                arrived(B1 + k, summed.at[d, place(sibling, k)], peer_s)
+                arrived(B2 + k, summed.at[other, place(sibling, k)], peer_s)
+            select(sibling * rows, rows)
+        if r == 1:
+            root_came(2)
+        select(across * rows + r * chunk, chunk)
+    root_came(3)
+    for r in range(CHUNKS):
         arrived(B3 + r, summed.at[d, place(far, r)], peer_s)
         arrived(B4 + r, summed.at[other, place(far, r)], peer_s)
-        select(far * rows + r * half, half)
+        select(far * rows + r * chunk, chunk)
     loads[3].wait()
 
     def tiled(body):
@@ -238,7 +264,8 @@
     loads[1].wait()
     for c in range(2):
         arrived(B5 + c, root_all.at[c, whole(sibling)], peer_s)
-        arrived(B6 + c, root_all.at[c, whole(far)], peer_s)
+    for k in range(4):
+        arrived(B6 + k, root_part(far, k), peer_s)
     for c in range(CAP):
 
         def multiply(i, total):
@@ -260,11 +287,9 @@
             gradient[c, whole(t)], gradient[c, cut], (((1,), (1,)), ((), ())),
             preferred_element_type=jnp.float32,
         )
-        left_buf[c, :, cut] = 0.95 * left_buf[c, :, cut] + 0.05 * product
+        left_out[c, :, cut] = 0.95 * left_out[c, :, cut] + 0.05 * product
 
     tiled(left)
-    stores.append(pltpu.make_async_copy(left_buf, left_out, out_sem.at[1]))
-    stores[1].start()
     loads[5].wait()
     window = pl.ds(pl.multiple_of(128 * ((3 * t) // 2), 128), tile)
     shift = pl.ds(pl.multiple_of(64 * (t % 2), 64), rows)
@@ -275,15 +300,26 @@
         product = jnp.dot(
             turned[c, shift], gradient[c, :, cut], preferred_element_type=jnp.float32
         )
-        right_buf[c, :, cut] = 0.95 * right_buf[c, :, cut] + 0.05 * product
+        right_out[c, :, cut] = 0.95 * right_out[c, :, cut] + 0.05 * product
 
     tiled(right)
-    stores.append(pltpu.make_async_copy(right_buf, right_out, out_sem.at[2]))
-    stores[2].start()
-
+    for copy in sent:
+        copy.wait_send()
     for k, (rank, peer) in enumerate(((sibling, peer_s), (across, peer_y), (far, peer_f))):
         arrived(Z + k, norms.at[rank], peer)
-    total = jnp.sum(norms[0] + norms[1] + norms[2] + norms[3], axis=1, keepdims=True)
+    totals[...] = norms[0] + norms[1] + norms[2] + norms[3]
+
+
+def finish(
+    left, right, second, precond, totals,
+    left_out, right_out, second_out, direction_out, direction, sems,
+):
+    rows = precond.shape[1]
+    pairs = ((left, left_out), (right, right_out), (second, second_out))
+    copies = [pltpu.make_async_copy(a, b, sems.at[k]) for k, (a, b) in enumerate(pairs)]
+    for copy in copies:
+        copy.start()
+    total = jnp.sum(totals[...], axis=1, keepdims=True)
     for c in range(CAP):
         scaling = jnp.sqrt(total[c : c + 1]) / jnp.sqrt(total[CAP + c : CAP + c + 1] + 1e-06)
 
@@ -293,11 +329,11 @@
             return carry
 
         lax.fori_loop(0, rows // 16, scale, 0, unroll=2)
-    stores.append(pltpu.make_async_copy(direction, direction_out, out_sem.at[3]))
-    stores[3].start()
-    for copy in sent:
-        copy.wait_send()
-    for copy in stores:
+        copies.append(
+            pltpu.make_async_copy(direction.at[c], direction_out.at[c], sems.at[3 + c])
+        )
+        copies[-1].start()
+    for copy in copies:
         copy.wait()
 
 
@@ -306,12 +342,13 @@
     full = (CAP, width, width)
     part = (CAP, rows, width)
     f32, bf16 = jnp.float32, jnp.bfloat16
-    anywhere = pl.BlockSpec(memory_space=pl.ANY)
-    outs = pl.pallas_call(
+    outside, inside = pl.BlockSpec(memory_space=pltpu.HBM), pl.BlockSpec(memory_space=pltpu.VMEM)
+    big, small = jax.ShapeDtypeStruct(part, f32), jax.ShapeDtypeStruct((8, 128), f32)
+    parts = pl.pallas_call(
         kernel,
-        out_shape=[jax.ShapeDtypeStruct(part, f32)] * 3 + [jax.ShapeDtypeStruct(part, bf16)],
-        in_specs=[pl.BlockSpec(memory_space=pltpu.SMEM)] + [anywhere] * 6,
-        out_specs=[anywhere] * 4,
+        out_shape=[big] * 4 + [small],
+        in_specs=[pl.BlockSpec(memory_space=pltpu.SMEM)] + [outside] * 6,
+        out_specs=[inside] * 5,
         scratch_shapes=[
             pltpu.VMEM((blocks, rows, width), bf16),
             pltpu.VMEM((blocks, rows, width), bf16),
@@ -319,26 +356,34 @@
             pltpu.VMEM(full, bf16),
             pltpu.VMEM(full, bf16),
             pltpu.VMEM(part, bf16),
-            pltpu.VMEM(part, f32),
-            pltpu.VMEM(part, f32),
-            pltpu.VMEM(part, f32),
-            pltpu.VMEM(part, bf16),
-            pltpu.VMEM(part, f32),
             pltpu.VMEM(part, bf16),
             pltpu.VMEM((CAP, 256, width), bf16),
             pltpu.VMEM((4, 8, 128), f32),
             pltpu.SemaphoreType.DMA((6,)),
-            pltpu.SemaphoreType.DMA((4,)),
             pltpu.SemaphoreType.DMA((Z + 3,)),
             pltpu.SemaphoreType.DMA((Z + 3,)),
         ],
         compiler_params=pltpu.CompilerParams(
-            collective_id=0, has_side_effects=True, vmem_limit_bytes=48 * 1024 * 1024
+            collective_id=0, has_side_effects=True, vmem_limit_bytes=32 * 1024 * 1024
         ),
     )(
-        owner, grads[0], left_stat[0, 0], right_stat[0, 0], second_moment[0, 0],
-        left_root[0, 0], right_root[0, 0],
+        owner.reshape(blocks),
+        *(
+            pltpu.with_memory_space_constraint(x, pltpu.HBM)
+            for x in (
+                grads[0], left_stat[0, 0], right_stat[0, 0], second_moment[0, 0],
+                left_root[0, 0], right_root[0, 0],
+            )
+        ),
     )
+    outs = pl.pallas_call(
+        finish,
+        out_shape=[big] * 3 + [jax.ShapeDtypeStruct(part, bf16)],
+        in_specs=[pl.BlockSpec(memory_space=pl.ANY)] * 3 + [inside] * 2,
+        out_specs=[outside] * 4,
+        scratch_shapes=[pltpu.VMEM(part, bf16), pltpu.SemaphoreType.DMA((3 + CAP,))],
+        compiler_params=pltpu.CompilerParams(vmem_limit_bytes=16 * 1024 * 1024),
+    )(*parts)
     return tuple(out[None, None] for out in outs)
 
 

time: 43.8 us -> 40.5 us (0.925); the launches traced: 43.1 us -> 40.4 us
  local copies, waits for them, and re-layouts: 7.79 us -> 0.65 us
  Pallas kernels: 34.7 us -> 39.1 us
    unnamed x11 -> x2, local copies, waits for them, and re-layouts: 7.79 us -> 0.65 us
    pallas_call x1 -> x2, Pallas kernels: 34.7 us -> 39.1 us  [the longest x1 37.1 us: fused_step(): pl.pallas_call(kernel, out_shape=[big] * 4 + [small], in_specs=[pl.BlockS...]
where the time goes in v2:
time: 40.5 us; the launch traced here: 40.4 us
  Pallas kernels  39.1 us (97%)
  local copies, waits for them, and re-layouts  0.65 us (2%)
  between operations  0.65 us (2%)
    pallas_call x1, Pallas kernels, fused_step(): pl.pallas_call(kernel, out_shape=[big] * 4 + [small], in_specs=[pl.BlockS...  37.1 us
    pallas_call x1, Pallas kernels, fused_step(): pl.pallas_call(finish, out_shape=[big] * 3 + [jax.ShapeDtypeStruct(part,...  2.02 us

profile of v2, /device:TPU:0, one launch (start us, length us, event | category | flops | bytes accessed | tf_op | source)
XLA Modules:
  0.0 40.4 jit_solution(14663072267312939315)
XLA Ops:
  0.6 0.0 copy-start
  0.6 0.6 %copy-done = s32[2,1]{0,1:T(1,128)S(1)} copy-done((s32[2,1]{0,1:T(1,128)S(1)}, s32[2,1]{0,1:T(1,128)}, u32[]{:S(2)}) %copy-start) | copy-done | bytes 32
  1.3 37.1 %shard_map.102 = (f32[2,192,768]{2,1,0:T(8,128)S(1)}, f32[2,192,768]{2,1,0:T(8,128)S(1)}, f32[2,192,768]{2,1,0:T(8,128)S(1)}, f32[2,192,768]{2,1,0:T(8,128)S(1)}, f32[8,128]{1,0:T(8,128)S(1)}) custom-call(s32[2]{0:T(128)S(1)} %bitcast.11, bf16[2,192,768]{2,1,0:T(8,128)(2,1)} %bitcast.15, f32[2,192,768]{2,1,0:T(8,128)} %bitcast.12, f32[2,192,768]{2,1,0:T(8,128)} %bitcast.13, ...), custom_call_target="tpu_custom_call" | custom-call | tf_op jit(solution)/shard_map/pallas_call | solution.py:347
  38.4 2.0 %shard_map.103 = (f32[2,192,768]{2,1,0:T(8,128)}, f32[2,192,768]{2,1,0:T(8,128)}, f32[2,192,768]{2,1,0:T(8,128)}, bf16[2,192,768]{2,1,0:T(8,128)(2,1)}) custom-call(f32[2,192,768]{2,1,0:T(8,128)S(1)} %get-tuple-element.13.left, f32[2,192,768]{2,1,0:T(8,128)S(1)} %get-tuple-element.14.right, f32[2,192,768]{2,1,0:T(8,128)S(1)} %get-tuple-element.15.second, ...), custom_call_target="tpu_custom_call" | custom-call | tf_op jit(solution)/shard_map/pallas_call | solution.py:379
Async XLA Ops:
  0.6 0.7 %copy-start = (s32[2,1]{0,1:T(1,128)S(1)}, s32[2,1]{0,1:T(1,128)}, u32[]{:S(2)}) copy-start(s32[2,1]{0,1:T(1,128)} %param.8) | copy-start | bytes 28

commit v3 on v2

--- a/solution.py
+++ b/solution.py
@@ -10,8 +10,8 @@
 CAP = 2
 MESH = pl.DeviceIdType.MESH
 
-CHUNKS = 4
-X1, X2, X3, Y1, Y2, B1, B2, B3, B4, B5, B6, Z = range(0, 12 * CHUNKS, CHUNKS)
+CHUNKS = 2
+X1, X2, X3, Y1, Y2, B4, B6, B1, B2, B3, B5, Z = (*range(0, 14, 2), *range(14, 19))
 
 
 def plain_step(grads, owner, left_stat, right_stat, second_moment, left_root, right_root):
@@ -68,15 +68,14 @@
 def fold(values):
     rows, columns = values.shape
     total = jnp.sum(values.reshape(rows // 8, 8, columns), axis=0)
-    total = sum(total[:, i : i + 128] for i in range(0, columns, 128))
-    return jnp.sum(total, axis=0, keepdims=True)
+    return sum(total[:, i : i + 128] for i in range(0, columns, 128))
 
 
 def kernel(
     owner, grads, left_stat, right_stat, second, left_root, right_root,
     left_out, right_out, second_out, precond, totals,
     mine, theirs, summed, gradient, root_all, root_left,
-    mixed, turned, norms, local_sem, send_sem, recv_sem,
+    mixed, turned, window_t, mixed_sum, right_sum, norms, local_sem, send_sem, recv_sem,
 ):
     d, t = lax.axis_index("dp"), lax.axis_index("tensor")
     blocks, rows, width = mine.shape
@@ -96,8 +95,8 @@
     def whole(rank):
         return pl.ds(pl.multiple_of(rank * rows, 16), rows)
 
-    def root_part(rank, k):
-        return root_all.at[k // 2, pl.ds(pl.multiple_of(rank * rows + k % 2 * half, 16), half)]
+    def root_part(rank, c):
+        return root_all.at[c, whole(rank)]
 
     def send(k, source, target, device):
         return pltpu.make_async_remote_copy(
@@ -120,13 +119,12 @@
         block, part = (other, d)[k // CHUNKS], pl.ds(k % CHUNKS * chunk, chunk)
         go(X1 + k, grads.at[block, part], theirs.at[block, part], peer_x)
 
-    def go_root(k):
-        source = right_root.at[k // 2, pl.ds(k % 2 * half, half)]
-        go(Y2 + k, source, root_part(t, k), peer_y)
-
-    def root_came(k):
-        arrived(Y2 + k, root_part(across, k), peer_y)
-        go(B6 + k, root_part(across, k), root_part(across, k), peer_s)
+    def go_root(c):
+        go(Y2 + c, right_root.at[c], root_part(t, c), peer_y)
+
+    def root_came(c):
+        arrived(Y2 + c, root_part(across, c), peer_y)
+        go(B6 + c, root_part(across, c), root_part(across, c), peer_s)
 
     sent = []
     norms[t] = jnp.zeros((8, 128), jnp.float32)
@@ -146,12 +144,13 @@
     pl.semaphore_wait(barrier, 4)
 
     go_x(0)
+    go_x(1)
     go_root(0)
-    go_x(1)
+    go_x(2)
+    go_x(3)
     for copy in loads[1:]:
         copy.start()
-    for c in range(2):
-        go(B5 + c, right_root.at[c], root_all.at[c, whole(t)], peer_s)
+    go(B5, right_root, root_all.at[:, whole(t)], peer_s)
 
     def add(block, r):
         def body(i, carry):
@@ -161,7 +160,7 @@
             summed[block, to] = total.astype(jnp.bfloat16)
             return carry
 
-        lax.fori_loop(0, chunk // 16, body, 0)
+        lax.fori_loop(0, chunk // 16, body, 0, unroll=3)
 
     owners = [owner[b] for b in range(blocks)]
     weights = []
@@ -184,35 +183,23 @@
                 gradient[c, at] = total.astype(jnp.bfloat16)
             return carry
 
-        lax.fori_loop(0, count // 16, body, 0)
-
-    def across_came(r):
-        arrived(Y1 + r, summed.at[d, place(across, r)], peer_y)
-        go_rows(X3 + r, d, place(across, r), peer_x)
-        go_rows(B3 + r, d, place(across, r), peer_s)
+        lax.fori_loop(0, count // 16, body, 0, unroll=3)
 
     loads[0].wait()
     for r in range(CHUNKS):
         arrived(X1 + r, theirs.at[d, pl.ds(r * chunk, chunk)], peer_x)
-        go_x(2 + r)
         add(d, r)
         go_rows(Y1 + r, d, place(t, r), peer_y)
-        go_rows(B1 + r, d, place(t, r), peer_s)
-        if r >= 2:
-            across_came(r - 2)
     go_root(1)
-    go_root(2)
+    go_rows(B1, d, whole(t), peer_s)
     for r in range(CHUNKS):
         arrived(X2 + r, theirs.at[other, pl.ds(r * chunk, chunk)], peer_x)
-        if 2 + CHUNKS + r < 2 * CHUNKS:
-            go_x(2 + CHUNKS + r)
         add(other, r)
-        go_rows(B2 + r, other, place(t, r), peer_s)
-        if r + CHUNKS - 2 < CHUNKS:
-            across_came(r + CHUNKS - 2)
-    root_came(0)
-    root_came(1)
-    go_root(3)
+        if r == CHUNKS - 1:
+            go_rows(B2, other, whole(t), peer_s)
+        arrived(Y1 + r, summed.at[d, place(across, r)], peer_y)
+        go_rows(X3 + r, d, place(across, r), peer_x)
+    go_rows(B3, d, whole(across), peer_s)
 
     select(t * rows, rows)
     loads[2].wait()
@@ -226,27 +213,16 @@
             adam = g / (jnp.sqrt(new) + 1e-08)
             return total + fold(adam * adam)
 
-        norms[t, c : c + 1] = lax.fori_loop(
-            0, rows // 16, moment, jnp.zeros((1, 128), jnp.float32)
+        norms[t, c : c + 1] = jnp.sum(
+            lax.fori_loop(0, rows // 16, moment, jnp.zeros((8, 128), jnp.float32), unroll=2),
+            axis=0, keepdims=True,
         )
-
-    for r in range(CHUNKS):
-        arrived(X3 + r, summed.at[other, place(across, r)], peer_x)
-        go_rows(B4 + r, other, place(across, r), peer_s)
-        if r == 0:
-            for k in range(CHUNKS):
-                arrived(B1 + k, summed.at[d, place(sibling, k)], peer_s)
-                arrived(B2 + k, summed.at[other, place(sibling, k)], peer_s)
-            select(sibling * rows, rows)
-        if r == 1:
-            root_came(2)
-        select(across * rows + r * chunk, chunk)
-    root_came(3)
-    for r in range(CHUNKS):
-        arrived(B3 + r, summed.at[d, place(far, r)], peer_s)
-        arrived(B4 + r, summed.at[other, place(far, r)], peer_s)
-        select(far * rows + r * chunk, chunk)
-    loads[3].wait()
+    root_came(0)
+
+    near = pl.ds(pl.multiple_of(t // 2 * 2 * rows, 128), 2 * rows)
+    away = pl.ds(pl.multiple_of((1 - t // 2) * 2 * rows, 128), 2 * rows)
+    window = pl.ds(pl.multiple_of(128 * ((3 * t) // 2), 128), tile)
+    shift = pl.ds(pl.multiple_of(64 * (t % 2), 64), rows)
 
     def tiled(body):
         def step(i, carry):
@@ -255,54 +231,81 @@
 
         lax.fori_loop(0, CAP * tiles, step, 0)
 
-    def mix(c, cut):
-        mixed[c, :, cut] = jnp.dot(
-            root_left[c], gradient[c, :, cut], preferred_element_type=jnp.float32
-        ).astype(jnp.bfloat16)
-
-    tiled(mix)
+    def turn(at):
+        for c in range(CAP):
+            window_t[c, :, at] = gradient[c, at, window].T
+            turned[c, :, at] = window_t[c, shift, at]
+
+    def left(at):
+        def step(c, carry):
+            product = lax.dot_general(
+                gradient[c, whole(t)], gradient[c, at], (((1,), (1,)), ((), ())),
+                preferred_element_type=jnp.float32,
+            )
+            left_out[c, :, at] = 0.95 * left_out[c, :, at] + 0.05 * product
+            return carry
+
+        lax.fori_loop(0, CAP, step, 0)
+
+    def dot(a, b):
+        return jnp.dot(a, b, preferred_element_type=jnp.float32)
+
+    def mix_near(c, cut):
+        mixed_sum[c, :, cut] = dot(root_left[c, :, near], gradient[c, near, cut])
+
+    def mix_away(c, cut):
+        product = dot(root_left[c, :, away], gradient[c, away, cut])
+        mixed[c, :, cut] = (mixed_sum[c, :, cut] + product).astype(jnp.bfloat16)
+
+    def right_near(c, cut):
+        right_sum[c, :, cut] = dot(turned[c, :, near], gradient[c, near, cut])
+
+    def right_away(c, cut):
+        product = right_sum[c, :, cut] + dot(turned[c, :, away], gradient[c, away, cut])
+        right_out[c, :, cut] = 0.95 * right_out[c, :, cut] + 0.05 * product
+
+    arrived(B1, summed.at[d, whole(sibling)], peer_s)
+    arrived(B2, summed.at[other, whole(sibling)], peer_s)
+    select(sibling * rows, rows)
+    loads[3].wait()
+    tiled(mix_near)
+    for r in range(CHUNKS):
+        arrived(X3 + r, summed.at[other, place(across, r)], peer_x)
+        go_rows(B4 + r, other, place(across, r), peer_s)
+        select(across * rows + r * chunk, chunk)
+        if r == 0:
+            turn(near)
+            tiled(right_near)
+            loads[4].wait()
+            left(near)
+    arrived(B3, summed.at[d, whole(far)], peer_s)
+    for r in range(CHUNKS):
+        arrived(B4 + r, summed.at[other, place(far, r)], peer_s)
+        select(far * rows + r * chunk, chunk)
+    root_came(1)
+    tiled(mix_away)
     loads[1].wait()
-    for c in range(2):
-        arrived(B5 + c, root_all.at[c, whole(sibling)], peer_s)
-    for k in range(4):
-        arrived(B6 + k, root_part(far, k), peer_s)
+    arrived(B5, root_all.at[:, whole(sibling)], peer_s)
     for c in range(CAP):
+        arrived(B6 + c, root_part(far, c), peer_s)
 
         def multiply(i, total):
             cut = pl.ds(pl.multiple_of(i * tile, tile), tile)
-            product = jnp.dot(mixed[c], root_all[c, :, cut], preferred_element_type=jnp.float32)
+            product = dot(mixed[c], root_all[c, :, cut])
             precond[c, :, cut] = product
             return total + fold(product * product)
 
-        norms[t, CAP + c : CAP + c + 1] = lax.fori_loop(
-            0, tiles, multiply, jnp.zeros((1, 128), jnp.float32)
+        norms[t, CAP + c : CAP + c + 1] = jnp.sum(
+            lax.fori_loop(0, tiles, multiply, jnp.zeros((8, 128), jnp.float32)),
+            axis=0, keepdims=True,
         )
     for k, peer in enumerate((peer_s, peer_y, peer_f)):
         go(Z + k, norms.at[t], norms.at[t], peer)
 
-    loads[4].wait()
-
-    def left(c, cut):
-        product = lax.dot_general(
-            gradient[c, whole(t)], gradient[c, cut], (((1,), (1,)), ((), ())),
-            preferred_element_type=jnp.float32,
-        )
-        left_out[c, :, cut] = 0.95 * left_out[c, :, cut] + 0.05 * product
-
-    tiled(left)
+    left(away)
+    turn(away)
     loads[5].wait()
-    window = pl.ds(pl.multiple_of(128 * ((3 * t) // 2), 128), tile)
-    shift = pl.ds(pl.multiple_of(64 * (t % 2), 64), rows)
-    for c in range(CAP):
-        turned[c] = gradient[c, :, window].T
-
-    def right(c, cut):
-        product = jnp.dot(
-            turned[c, shift], gradient[c, :, cut], preferred_element_type=jnp.float32
-        )
-        right_out[c, :, cut] = 0.95 * right_out[c, :, cut] + 0.05 * product
-
-    tiled(right)
+    tiled(right_away)
     for copy in sent:
         copy.wait_send()
     for k, (rank, peer) in enumerate(((sibling, peer_s), (across, peer_y), (far, peer_f))):
@@ -357,7 +360,10 @@
             pltpu.VMEM(full, bf16),
             pltpu.VMEM(part, bf16),
             pltpu.VMEM(part, bf16),
+            pltpu.VMEM(part, bf16),
             pltpu.VMEM((CAP, 256, width), bf16),
+            pltpu.VMEM(part, f32),
+            pltpu.VMEM(part, f32),
             pltpu.VMEM((4, 8, 128), f32),
             pltpu.SemaphoreType.DMA((6,)),
             pltpu.SemaphoreType.DMA((Z + 3,)),

time: 40.5 us -> 35.3 us (0.87); the launches traced: 40.4 us -> 34.8 us
  Pallas kernels: 39.1 us -> 33.5 us
    pallas_call x1, Pallas kernels: 37.1 us -> 31.5 us  [fused_step(): pl.pallas_call(kernel, out_shape=[big] * 4 + [small], in_specs=[pl.BlockS...]
where the time goes in v3:
time: 35.3 us; the launch traced here: 34.8 us
  Pallas kernels  33.5 us (95%)
  local copies, waits for them, and re-layouts  0.65 us (2%)
  between operations  0.65 us (2%)
    pallas_call x1, Pallas kernels, fused_step(): pl.pallas_call(kernel, out_shape=[big] * 4 + [small], in_specs=[pl.BlockS...  31.5 us
    pallas_call x1, Pallas kernels, fused_step(): pl.pallas_call(finish, out_shape=[big] * 3 + [jax.ShapeDtypeStruct(part,...  2.02 us

profile of v3, /device:TPU:0, one launch (start us, length us, event | category | flops | bytes accessed | tf_op | source)
XLA Modules:
  0.0 34.8 jit_solution(768773289045177988)
XLA Ops:
  0.6 0.0 copy-start
  0.6 0.6 %copy-done = s32[2,1]{0,1:T(1,128)S(1)} copy-done((s32[2,1]{0,1:T(1,128)S(1)}, s32[2,1]{0,1:T(1,128)}, u32[]{:S(2)}) %copy-start) | copy-done | bytes 32
  1.3 31.5 %shard_map.102 = (f32[2,192,768]{2,1,0:T(8,128)S(1)}, f32[2,192,768]{2,1,0:T(8,128)S(1)}, f32[2,192,768]{2,1,0:T(8,128)S(1)}, f32[2,192,768]{2,1,0:T(8,128)S(1)}, f32[8,128]{1,0:T(8,128)S(1)}) custom-call(s32[2]{0:T(128)S(1)} %bitcast.11, bf16[2,192,768]{2,1,0:T(8,128)(2,1)} %bitcast.15, f32[2,192,768]{2,1,0:T(8,128)} %bitcast.12, f32[2,192,768]{2,1,0:T(8,128)} %bitcast.13, ...), custom_call_target="tpu_custom_call" | custom-call | tf_op jit(solution)/shard_map/pallas_call | solution.py:350
  32.8 2.0 %shard_map.103 = (f32[2,192,768]{2,1,0:T(8,128)}, f32[2,192,768]{2,1,0:T(8,128)}, f32[2,192,768]{2,1,0:T(8,128)}, bf16[2,192,768]{2,1,0:T(8,128)(2,1)}) custom-call(f32[2,192,768]{2,1,0:T(8,128)S(1)} %get-tuple-element.13.left, f32[2,192,768]{2,1,0:T(8,128)S(1)} %get-tuple-element.14.right, f32[2,192,768]{2,1,0:T(8,128)S(1)} %get-tuple-element.15.second, ...), custom_call_target="tpu_custom_call" | custom-call | tf_op jit(solution)/shard_map/pallas_call | solution.py:385
Async XLA Ops:
  0.6 0.7 %copy-start = (s32[2,1]{0,1:T(1,128)S(1)}, s32[2,1]{0,1:T(1,128)}, u32[]{:S(2)}) copy-start(s32[2,1]{0,1:T(1,128)} %param.8) | copy-start | bytes 28

commit v4 on v3

--- a/solution.py
+++ b/solution.py
@@ -11,7 +11,7 @@
 MESH = pl.DeviceIdType.MESH
 
 CHUNKS = 2
-X1, X2, X3, Y1, Y2, B4, B6, B1, B2, B3, B5, Z = (*range(0, 14, 2), *range(14, 19))
+X1, X2, X3, Y1, B4, B6, B1, B2, B3, B5, Y2, Z = (*range(0, 12, 2), *range(12, 17), 20)
 
 
 def plain_step(grads, owner, left_stat, right_stat, second_moment, left_root, right_root):
@@ -119,11 +119,15 @@
         block, part = (other, d)[k // CHUNKS], pl.ds(k % CHUNKS * chunk, chunk)
         go(X1 + k, grads.at[block, part], theirs.at[block, part], peer_x)
 
-    def go_root(c):
-        go(Y2 + c, right_root.at[c], root_part(t, c), peer_y)
+    def root_half(rank, k):
+        return root_all.at[k // 2, pl.ds(pl.multiple_of(rank * rows + k % 2 * half, 16), half)]
+
+    def go_root(k):
+        go(Y2 + k, right_root.at[k // 2, pl.ds(k % 2 * half, half)], root_half(t, k), peer_y)
 
     def root_came(c):
-        arrived(Y2 + c, root_part(across, c), peer_y)
+        for k in (2 * c, 2 * c + 1):
+            arrived(Y2 + k, root_half(across, k), peer_y)
         go(B6 + c, root_part(across, c), root_part(across, c), peer_s)
 
     sent = []
@@ -146,8 +150,6 @@
     go_x(0)
     go_x(1)
     go_root(0)
-    go_x(2)
-    go_x(3)
     for copy in loads[1:]:
         copy.start()
     go(B5, right_root, root_all.at[:, whole(t)], peer_s)
@@ -188,17 +190,19 @@
     loads[0].wait()
     for r in range(CHUNKS):
         arrived(X1 + r, theirs.at[d, pl.ds(r * chunk, chunk)], peer_x)
+        go_x(CHUNKS + r)
         add(d, r)
         go_rows(Y1 + r, d, place(t, r), peer_y)
-    go_root(1)
     go_rows(B1, d, whole(t), peer_s)
     for r in range(CHUNKS):
+        arrived(Y1 + r, summed.at[d, place(across, r)], peer_y)
+        go_rows(X3 + r, d, place(across, r), peer_x)
+        go_root(1 + r)
+        if r == CHUNKS - 1:
+            go_root(3)
         arrived(X2 + r, theirs.at[other, pl.ds(r * chunk, chunk)], peer_x)
         add(other, r)
-        if r == CHUNKS - 1:
-            go_rows(B2, other, whole(t), peer_s)
-        arrived(Y1 + r, summed.at[d, place(across, r)], peer_y)
-        go_rows(X3 + r, d, place(across, r), peer_x)
+    go_rows(B2, other, whole(t), peer_s)
     go_rows(B3, d, whole(across), peer_s)
 
     select(t * rows, rows)

time: 35.3 us -> 36.2 us (1.025); the launches traced: 34.8 us -> 36.1 us
  Pallas kernels: 33.5 us -> 34.8 us
    pallas_call x1, Pallas kernels: 31.5 us -> 32.7 us  [fused_step(): pl.pallas_call(kernel, out_shape=[big] * 4 + [small], in_specs=[pl.BlockS...]
where the time goes in v4:
time: 36.2 us; the launch traced here: 36.1 us
  Pallas kernels  34.8 us (96%)
  local copies, waits for them, and re-layouts  0.65 us (2%)
  between operations  0.65 us (2%)
    pallas_call x1, Pallas kernels, fused_step(): pl.pallas_call(kernel, out_shape=[big] * 4 + [small], in_specs=[pl.BlockS...  32.7 us
    pallas_call x1, Pallas kernels, fused_step(): pl.pallas_call(finish, out_shape=[big] * 3 + [jax.ShapeDtypeStruct(part,...  2.02 us

profile of v4, /device:TPU:0, one launch (start us, length us, event | category | flops | bytes accessed | tf_op | source)
XLA Modules:
  0.0 36.1 jit_solution(8276931529587205821)
XLA Ops:
  0.6 0.0 copy-start
  0.6 0.6 %copy-done = s32[2,1]{0,1:T(1,128)S(1)} copy-done((s32[2,1]{0,1:T(1,128)S(1)}, s32[2,1]{0,1:T(1,128)}, u32[]{:S(2)}) %copy-start) | copy-done | bytes 32
  1.3 32.7 %shard_map.102 = (f32[2,192,768]{2,1,0:T(8,128)S(1)}, f32[2,192,768]{2,1,0:T(8,128)S(1)}, f32[2,192,768]{2,1,0:T(8,128)S(1)}, f32[2,192,768]{2,1,0:T(8,128)S(1)}, f32[8,128]{1,0:T(8,128)S(1)}) custom-call(s32[2]{0:T(128)S(1)} %bitcast.11, bf16[2,192,768]{2,1,0:T(8,128)(2,1)} %bitcast.15, f32[2,192,768]{2,1,0:T(8,128)} %bitcast.12, f32[2,192,768]{2,1,0:T(8,128)} %bitcast.13, ...), custom_call_target="tpu_custom_call" | custom-call | tf_op jit(solution)/shard_map/pallas_call | solution.py:354
  34.0 2.0 %shard_map.103 = (f32[2,192,768]{2,1,0:T(8,128)}, f32[2,192,768]{2,1,0:T(8,128)}, f32[2,192,768]{2,1,0:T(8,128)}, bf16[2,192,768]{2,1,0:T(8,128)(2,1)}) custom-call(f32[2,192,768]{2,1,0:T(8,128)S(1)} %get-tuple-element.13.left, f32[2,192,768]{2,1,0:T(8,128)S(1)} %get-tuple-element.14.right, f32[2,192,768]{2,1,0:T(8,128)S(1)} %get-tuple-element.15.second, ...), custom_call_target="tpu_custom_call" | custom-call | tf_op jit(solution)/shard_map/pallas_call | solution.py:389
Async XLA Ops:
  0.6 0.7 %copy-start = (s32[2,1]{0,1:T(1,128)S(1)}, s32[2,1]{0,1:T(1,128)}, u32[]{:S(2)}) copy-start(s32[2,1]{0,1:T(1,128)} %param.8) | copy-start | bytes 28

commit v5 on v3

--- a/solution.py
+++ b/solution.py
@@ -11,7 +11,7 @@
 MESH = pl.DeviceIdType.MESH
 
 CHUNKS = 2
-X1, X2, X3, Y1, Y2, B4, B6, B1, B2, B3, B5, Z = (*range(0, 14, 2), *range(14, 19))
+X1, X2, X3, Y1, B4, B6, B1, B2, B3, B5, Y3, Y2, Z = (*range(0, 12, 2), *range(12, 18), 20)
 
 
 def plain_step(grads, owner, left_stat, right_stat, second_moment, left_root, right_root):
@@ -75,7 +75,7 @@
     owner, grads, left_stat, right_stat, second, left_root, right_root,
     left_out, right_out, second_out, precond, totals,
     mine, theirs, summed, gradient, root_all, root_left,
-    mixed, turned, window_t, mixed_sum, right_sum, norms, local_sem, send_sem, recv_sem,
+    mixed, turned, window_t, mixed_sum, right_sum, norms, owner_at, local_sem, send_sem, recv_sem,
 ):
     d, t = lax.axis_index("dp"), lax.axis_index("tensor")
     blocks, rows, width = mine.shape
@@ -119,12 +119,23 @@
         block, part = (other, d)[k // CHUNKS], pl.ds(k % CHUNKS * chunk, chunk)
         go(X1 + k, grads.at[block, part], theirs.at[block, part], peer_x)
 
-    def go_root(c):
-        go(Y2 + c, right_root.at[c], root_part(t, c), peer_y)
+    def root_piece(rank, k):
+        if k == 0:
+            return root_part(rank, 0)
+        at = pl.ds(pl.multiple_of(rank * rows + (k - 1) * half, 16), half)
+        return root_all.at[1, at]
+
+    def go_root(k):
+        source = right_root.at[0] if k == 0 else right_root.at[1, pl.ds((k - 1) * half, half)]
+        go(Y2 + k, source, root_piece(t, k), peer_y)
 
     def root_came(c):
-        arrived(Y2 + c, root_part(across, c), peer_y)
+        for k in ((0,), (1, 2))[c]:
+            arrived(Y2 + k, root_piece(across, k), peer_y)
         go(B6 + c, root_part(across, c), root_part(across, c), peer_s)
+
+    def quarter(rank, k):
+        return pl.ds(pl.multiple_of(rank * rows + k * (chunk // 2), 16), chunk // 2)
 
     sent = []
     norms[t] = jnp.zeros((8, 128), jnp.float32)
@@ -135,8 +146,10 @@
         load(3, left_root, root_left),
         load(4, left_stat, left_out),
         load(5, right_stat, right_out),
+        load(6, owner, owner_at),
     ]
     loads[0].start()
+    loads[6].start()
 
     barrier = pltpu.get_barrier_semaphore()
     for peer in (peer_x, peer_s, peer_y, peer_f):
@@ -148,7 +161,7 @@
     go_root(0)
     go_x(2)
     go_x(3)
-    for copy in loads[1:]:
+    for copy in loads[1:6]:
         copy.start()
     go(B5, right_root, root_all.at[:, whole(t)], peer_s)
 
@@ -162,7 +175,8 @@
 
         lax.fori_loop(0, chunk // 16, body, 0, unroll=3)
 
-    owners = [owner[b] for b in range(blocks)]
+    loads[6].wait()
+    owners = [owner_at[b] for b in range(blocks)]
     weights = []
     for c in range(CAP):
         row = []
@@ -197,8 +211,10 @@
         add(other, r)
         if r == CHUNKS - 1:
             go_rows(B2, other, whole(t), peer_s)
+            go_rows(Y3, other, quarter(t, 3), peer_y)
+            go_root(2)
         arrived(Y1 + r, summed.at[d, place(across, r)], peer_y)
-        go_rows(X3 + r, d, place(across, r), peer_x)
+        go_rows(X3 + r, d, place(across, 0) if r == 0 else quarter(across, 2), peer_x)
     go_rows(B3, d, whole(across), peer_s)
 
     select(t * rows, rows)
@@ -270,7 +286,10 @@
     loads[3].wait()
     tiled(mix_near)
     for r in range(CHUNKS):
-        arrived(X3 + r, summed.at[other, place(across, r)], peer_x)
+        at = place(across, 0) if r == 0 else quarter(across, 2)
+        arrived(X3 + r, summed.at[other, at], peer_x)
+        if r == 1:
+            arrived(Y3, summed.at[other, quarter(across, 3)], peer_y)
         go_rows(B4 + r, other, place(across, r), peer_s)
         select(across * rows + r * chunk, chunk)
         if r == 0:
@@ -282,11 +301,13 @@
     for r in range(CHUNKS):
         arrived(B4 + r, summed.at[other, place(far, r)], peer_s)
         select(far * rows + r * chunk, chunk)
-    root_came(1)
     tiled(mix_away)
     loads[1].wait()
     arrived(B5, root_all.at[:, whole(sibling)], peer_s)
     for c in range(CAP):
+        if c == 1:
+            left(away)
+            root_came(1)
         arrived(B6 + c, root_part(far, c), peer_s)
 
         def multiply(i, total):
@@ -302,7 +323,6 @@
     for k, peer in enumerate((peer_s, peer_y, peer_f)):
         go(Z + k, norms.at[t], norms.at[t], peer)
 
-    left(away)
     turn(away)
     loads[5].wait()
     tiled(right_away)
@@ -350,7 +370,7 @@
     parts = pl.pallas_call(
         kernel,
         out_shape=[big] * 4 + [small],
-        in_specs=[pl.BlockSpec(memory_space=pltpu.SMEM)] + [outside] * 6,
+        in_specs=[outside] * 7,
         out_specs=[inside] * 5,
         scratch_shapes=[
             pltpu.VMEM((blocks, rows, width), bf16),
@@ -365,7 +385,8 @@
             pltpu.VMEM(part, f32),
             pltpu.VMEM(part, f32),
             pltpu.VMEM((4, 8, 128), f32),
-            pltpu.SemaphoreType.DMA((6,)),
+            pltpu.SMEM((blocks,), jnp.int32),
+            pltpu.SemaphoreType.DMA((7,)),
             pltpu.SemaphoreType.DMA((Z + 3,)),
             pltpu.SemaphoreType.DMA((Z + 3,)),
         ],
@@ -373,11 +394,10 @@
             collective_id=0, has_side_effects=True, vmem_limit_bytes=32 * 1024 * 1024
         ),
     )(
-        owner.reshape(blocks),
         *(
             pltpu.with_memory_space_constraint(x, pltpu.HBM)
             for x in (
-                grads[0], left_stat[0, 0], right_stat[0, 0], second_moment[0, 0],
+                owner.reshape(blocks), grads[0], left_stat[0, 0], right_stat[0, 0], second_moment[0, 0],
                 left_root[0, 0], right_root[0, 0],
             )
         ),

time: 35.3 us -> 36 us (1.020)
  Pallas kernels: 33.5 us -> 35.2 us
  local copies, waits for them, and re-layouts: 0.65 us -> 0 us
    pallas_call x1, Pallas kernels: 31.5 us -> 33.2 us  [fused_step(): pl.pallas_call(kernel, out_shape=[big] * 4 + [small], in_specs=[outside]...]
    unnamed x2 -> x0, local copies, waits for them, and re-layouts: 0.65 us -> none
where the time goes in v5:
time: 36 us; the launch traced here: 35.8 us
  Pallas kernels  35.2 us (98%)
  between operations  0.64 us (2%)
    pallas_call x1, Pallas kernels, fused_step(): pl.pallas_call(kernel, out_shape=[big] * 4 + [small], in_specs=[outside]...  33.2 us
    pallas_call x1, Pallas kernels, fused_step(): pl.pallas_call(finish, out_shape=[big] * 3 + [jax.ShapeDtypeStruct(part,...  2.02 us

profile of v5, /device:TPU:0, one launch (start us, length us, event | category | flops | bytes accessed | tf_op | source)
XLA Modules:
  0.0 35.8 jit_solution(15311455739235383070)
XLA Ops:
  0.6 33.2 %shard_map.102 = (f32[2,192,768]{2,1,0:T(8,128)S(1)}, f32[2,192,768]{2,1,0:T(8,128)S(1)}, f32[2,192,768]{2,1,0:T(8,128)S(1)}, f32[2,192,768]{2,1,0:T(8,128)S(1)}, f32[8,128]{1,0:T(8,128)S(1)}) custom-call(s32[2]{0:T(128)} %bitcast.17, bf16[2,192,768]{2,1,0:T(8,128)(2,1)} %bitcast.14, f32[2,192,768]{2,1,0:T(8,128)} %bitcast.11, f32[2,192,768]{2,1,0:T(8,128)} %bitcast.12, ...), custom_call_target="tpu_custom_call" | custom-call | tf_op jit(solution)/shard_map/pallas_call | solution.py:370
  33.8 2.0 %shard_map.103 = (f32[2,192,768]{2,1,0:T(8,128)}, f32[2,192,768]{2,1,0:T(8,128)}, f32[2,192,768]{2,1,0:T(8,128)}, bf16[2,192,768]{2,1,0:T(8,128)(2,1)}) custom-call(f32[2,192,768]{2,1,0:T(8,128)S(1)} %get-tuple-element.13.left, f32[2,192,768]{2,1,0:T(8,128)S(1)} %get-tuple-element.14.right, f32[2,192,768]{2,1,0:T(8,128)S(1)} %get-tuple-element.15.second, ...), custom_call_target="tpu_custom_call" | custom-call | tf_op jit(solution)/shard_map/pallas_call | solution.py:405
